TPU v7x, 512 devices: a whole 4x4x16 slice. The times are simulated.
512 devices in a mesh: space: 32 (over z, core), tm: 16 (over x, y).
Axes of the slice: x: 4, y: 4, z: 16, core: 2. Of those that a mesh axis runs over, the one named last changes fastest.
Arguments:
- recordings: bfloat16 [2, 3, 512, 32768], P(None, None, 'space', 'tm'), may hold values from -30 to 30
- owner: int32 [512, 1], P('space'), may hold values from 0 to 31; in each aligned block of 16 rows (0 to 15, 16 to 31, ...) at most 2 rows name the same one
- valid_range: int32 [512, 2], P('space'), may hold values from 0 to 32768, as said below
- bin_mask: int32 [512, 96], P('space'), may hold values 0 or 1
Outputs:
- adjoint: bfloat16 [3, 2048, 32768], P(None, 'space', 'tm')
Inputs may be any that keep to these rules, and one draw needn't show every extreme that they name: `owner`: among the 16 receivers listed on one index of space, no subdomain owns more than 2; some subdomain owns exactly 2 of them. `valid_range`: column 0 is below column 1 in every row.
All inputs are finite; a program needn't handle non-finite values. No bound on the sum of `bin_mask` on one device may be relied on, other than what follows from the above.
Results may differ from a plain program's by a relative error of at most 0.013.
Values may be sent and summed in bfloat16 or wider, within the bound.
A program may use at most 128 MiB of HBM per device.

v0:
```python
import math
import jax
import jax.numpy as jnp
from jax import lax
from jax.sharding import PartitionSpec as P

BINS = 96
HOP = 256
HALO = 1024
KERNEL = 2304
WATER = 0.1
EPSILON = 1e-06


def with_halo(block, sides, width):
    for axis, dim in sides:
        count = lax.axis_size(axis)
        forward = [(i, i + 1) for i in range(count - 1)]
        backward = [(target, source) for source, target in forward]
        low = lax.ppermute(
            lax.slice_in_dim(block, block.shape[dim] - width, None, axis=dim), axis, forward
        )
        high = lax.ppermute(lax.slice_in_dim(block, 0, width, axis=dim), axis, backward)
        block = jnp.concatenate([low, block, high], axis=dim)
    return block


def shifted(block, axis, distance):
    devices = range(lax.axis_size(axis))
    route = [(i - distance, i) for i in devices if i - distance in devices]
    return lax.ppermute(block, axis, route)


def cq_kernel(kern_len, bins):
    octave_bins = bins // 8
    index = jnp.arange(bins).astype(jnp.float32)
    freq = 0.25 * jnp.exp2((index - (bins - 1)) / octave_bins)
    quality = 1.0 / (2.0 ** (1.0 / octave_bins) - 1.0)
    support = jnp.minimum(quality / freq, float(kern_len))
    offset = jnp.arange(kern_len).astype(jnp.float32) - 0.5 * (kern_len - 1)
    ratio = offset[:, None] / support[None, :]
    window = jnp.where(jnp.abs(ratio) < 0.5, 0.5 + 0.5 * jnp.cos(2.0 * math.pi * ratio), 0.0)
    window = window / jnp.sqrt(jnp.sum(window * window, axis=0, keepdims=True))
    cycles = offset[:, None] * freq[None, :]
    phase = cycles - jnp.floor(cycles)
    table = jnp.concatenate(
        [window * jnp.cos(2.0 * math.pi * phase), -window * jnp.sin(2.0 * math.pi * phase)], axis=1
    )
    return table.astype(jnp.bfloat16)


def adjoint_of(syn_re, syn_im, obs_re, obs_im, weight):
    level = (
        WATER * jnp.mean(obs_re * obs_re + obs_im * obs_im, axis=(-2, -1), keepdims=True) + EPSILON
    )
    syn_norm = jnp.sqrt(syn_re * syn_re + syn_im * syn_im + level)
    obs_norm = jnp.sqrt(obs_re * obs_re + obs_im * obs_im + level)
    diff_re = weight * (syn_re / syn_norm - obs_re / obs_norm)
    diff_im = weight * (syn_im / syn_norm - obs_im / obs_norm)
    inner = (syn_re * diff_re + syn_im * diff_im) / (syn_norm * syn_norm * syn_norm)
    return (diff_re / syn_norm - syn_re * inner, diff_im / syn_norm - syn_im * inner)


def analyse(blocks, table, frames):
    taps = table.shape[0] // HOP
    unfolded = jnp.concatenate([blocks[..., tap : tap + frames, :] for tap in range(taps)], axis=-1)
    return jnp.einsum("...fh,hk->...fk", unfolded, table, preferred_element_type=jnp.float32)


def synthesise(coefs, table, frames):
    taps = table.shape[0] // HOP
    term = jnp.einsum("...fk,hk->...fh", coefs, table, preferred_element_type=jnp.float32)
    term = term.reshape(term.shape[:-1] + (taps, HOP))
    lead = len(term.shape) - 3
    ext = jnp.zeros(coefs.shape[:-2] + (frames + taps - 1, HOP), jnp.float32)
    for tap in range(taps):
        widths = [(0, 0)] * lead + [(tap, taps - 1 - tap), (0, 0)]
        ext = ext + jnp.pad(term[..., tap, :], widths)
    return ext


def frame_weight(ranges, masks, frames_all):
    centers = jnp.arange(frames_all, dtype=jnp.int32) * HOP + HOP // 2
    inside = (ranges[:, 0:1] <= centers[None, :]) & (centers[None, :] < ranges[:, 1:2])
    return inside.astype(jnp.float32)[:, :, None] * masks.astype(jnp.float32)[:, None, :]


def misfit(coefs, weight):
    adj_re, adj_im = adjoint_of(
        coefs[0, ..., :BINS],
        coefs[0, ..., BINS:],
        coefs[1, ..., :BINS],
        coefs[1, ..., BINS:],
        weight,
    )
    joined = jnp.concatenate([adj_re, adj_im], axis=-1)
    return joined.reshape(joined.shape[:2] + (joined.shape[2] * joined.shape[3],)).astype(
        jnp.bfloat16
    )


def on_device(recordings, owner, valid_range, bin_mask):
    table = cq_kernel(KERNEL, BINS)
    margin = HALO // HOP
    width = 2 * BINS
    groups = lax.axis_size("tm")
    comps = recordings.shape[1]
    rec_dev = recordings.shape[2]
    samples_dev = recordings.shape[3]
    frames_dev = samples_dev // HOP
    rec_group = rec_dev // groups
    first_row = lax.axis_index("tm") * rec_group
    ranges = lax.dynamic_slice_in_dim(valid_range, first_row, rec_group, 0)
    masks = lax.dynamic_slice_in_dim(bin_mask, first_row, rec_group, 0)
    extended = with_halo(recordings, (("tm", 3),), HALO)
    blocks = extended.reshape(2, comps, rec_dev, frames_dev + 2 * margin, HOP)
    coefs = analyse(blocks, table, frames_dev)
    packed = coefs.astype(jnp.bfloat16).reshape(2, comps, rec_dev, frames_dev * width)
    weight = frame_weight(ranges, masks, frames_dev * groups)
    pieces = lax.all_to_all(packed, "tm", split_axis=2, concat_axis=3, tiled=True)
    items = pieces.shape[1]
    frames_all = pieces.shape[3] // width
    local_coefs = pieces.astype(jnp.float32).reshape(2, items, rec_group, frames_all, width)
    adjoint_local = misfit(local_coefs, weight)
    adjoint_back = lax.all_to_all(adjoint_local, "tm", split_axis=2, concat_axis=1, tiled=True)
    adjoint_frames = adjoint_back.reshape(comps, rec_dev, frames_dev, width)
    ext = synthesise(adjoint_frames, table, frames_dev)
    flat = ext.reshape(comps, rec_dev, (frames_dev + 2 * margin) * HOP)
    middle = flat[:, :, HALO : HALO + samples_dev]
    from_before = shifted(flat[:, :, HALO + samples_dev :].astype(jnp.bfloat16), "tm", 1).astype(
        jnp.float32
    )
    from_after = shifted(flat[:, :, :HALO].astype(jnp.bfloat16), "tm", -1).astype(jnp.float32)
    middle = middle.at[:, :, :HALO].add(from_before)
    middle = middle.at[:, :, samples_dev - HALO :].add(from_after)
    series = middle.astype(jnp.bfloat16)
    count = lax.axis_size("space")
    most = max(2, 3 * rec_dev // (2 * count))
    target = owner[:, 0]
    place = jnp.arange(rec_dev, dtype=jnp.int32)
    earlier = (target[:, None] == target[None, :]) & (place[None, :] < place[:, None])
    rank = jnp.sum(earlier.astype(jnp.int32), axis=1)
    slot = target * most + rank
    select = (jnp.arange(count * most, dtype=jnp.int32)[:, None] == slot[None, :]).astype(
        jnp.bfloat16
    )
    outgoing = jnp.einsum("sr,crt->cst", select, series, preferred_element_type=jnp.float32).astype(
        jnp.bfloat16
    )
    return lax.all_to_all(outgoing, "space", split_axis=1, concat_axis=1, tiled=True)


def solution(mesh):
    return jax.shard_map(
        on_device,
        mesh=mesh,
        in_specs=(
            P(None, None, "space", "tm"),
            P("space", None),
            P("space", None),
            P("space", None),
        ),
        out_specs=P(None, "space", "tm"),
        check_vma=False,
    )
```

profile of v0, /device:TPU:25, one launch (start us, length us, event | category | flops | bytes accessed | tf_op | source)
XLA Modules:
  0.0 341.8 jit_solution(2724905111548227926)
XLA Ops:
  0.0 1.1 fusion.24
  1.1 2.8 collective-permute-start
  3.9 2.5 collective-permute-start.1
  6.4 3.4 %multiply_reduce_fusion = f32[96]{0:T(128)S(1)} fusion(f32[96]{0:T(128)S(1)} %get-tuple-element.50, f32[2304]{0:T(1024)S(1)} %convert_add_fusion.1), kind=kLoop, calls=%fused_computation.20 | loop fusion | flops 1990560 | bytes 9984 | tf_op jit(solution)/shard_map/reduce_sum | solution.py:43
  9.9 0.6 fusion.25
  10.5 6.6 %multiply_convert_fusion.3 = (bf16[2304,96]{0,1:T(8,128)(2,1)S(1)}, bf16[2304,96]{0,1:T(8,128)(2,1)S(1)}) fusion(f32[96]{0:T(128)S(1)} %get-tuple-element.51, f32[2304]{0:T(1024)S(1)} %convert_add_fusion.1, f32[96]{0:T(128)S(1)} %sqrt.38, f32[96]{0:T(128)S(1)} %get-tuple-element.50), kind=kLoop, calls=%fused_computation.19 | loop fusion | flops 3760128 | bytes 895104 | tf_op jit(solution)/shard_map/convert.7
  17.2 0.7 fusion.19
  17.9 1.1 pad_maximum_fusion
  19.0 0.2 copy.106
  19.2 0.1 slice_dynamic-update-slice_fusion.7
  19.3 0.1 slice_dynamic-update-slice_fusion.6
  19.4 0.1 slice_dynamic-update-slice_fusion.5
  19.6 0.1 slice_dynamic-update-slice_fusion.4
  19.7 0.1 slice_dynamic-update-slice_fusion.3
  19.8 0.1 slice_dynamic-update-slice_fusion.2
  19.9 0.1 slice_dynamic-update-slice_fusion.1
  20.1 1.1 convolution_convert_fusion.1
  21.2 0.3 reshape.521
  21.6 1.0 copy.78
  22.6 6.6 %all-to-all-start = ((bf16[2,3,16,1536]{3,0,1,2:T(2,128)(2,1)}), bf16[2,3,16,1536]{3,0,1,2:T(2,128)(2,1)S(1)}, u32[]{:S(2)}, u32[]{:S(2)}) async-start(bf16[2,3,16,1536]{3,0,1,2:T(2,128)(2,1)} %copy.78), calls=%async_computation | async-start | bytes 589824 | tf_op jit(solution)/shard_map/all_to_all | solution.py:120
  29.2 1.3 and_convert_fusion
  30.5 4.4 %all-to-all-done = bf16[2,3,16,1536]{3,0,1,2:T(2,128)(2,1)S(1)} async-done(((bf16[2,3,16,1536]{3,0,1,2:T(2,128)(2,1)}), bf16[2,3,16,1536]{3,0,1,2:T(2,128)(2,1)S(1)}, u32[]{:S(2)}, u32[]{:S(2)}) %all-to-all-start) | async-done | bytes 294944 | tf_op jit(solution)/shard_map/all_to_all | solution.py:120
  34.9 0.2 reshape.524
  35.2 0.2 fusion.22
  35.4 0.4 subtract_convert_fusion.1
  35.8 0.1 pad_maximum_fusion.1
  35.9 0.2 convert_element_type.135
  36.2 19.4 %copy.83 = bf16[3,1,24576]{0,1,2:T(2,128)(2,1)} copy(bf16[3,1,24576]{2,0,1:T(4,128)(2,1)S(1)} %convert_element_type.135) | data formatting | bytes 294912 | tf_op jit(solution)/shard_map/convert_element_type | solution.py:97
  55.6 0.5 broadcast.336
  56.1 135.0 %reduce.5 = bf16[24576,3]{1,0:T(8,128)(2,1)} reduce(bf16[24576,1,3]{2,1,0:T(2,128)(2,1)} %bitcast.152, bf16[]{:T(256)} %broadcast.336), dimensions={1}, to_apply=%bitcast.148.reduce_sub_computation | reduce | bytes 294914
  191.1 10.0 %reshape.530 = bf16[16,2,2304]{2,1,0:T(2,128)(2,1)} reshape(bf16[24576,3]{1,0:T(8,128)(2,1)} %reduce.5) | data formatting | bytes 294912
  201.1 5.5 %all-to-all-start.1 = ((bf16[16,2,2304]{2,1,0:T(2,128)(2,1)}), bf16[16,2,2304]{2,1,0:T(2,128)(2,1)S(1)}, u32[]{:S(2)}, u32[]{:S(2)}) async-start(bf16[16,2,2304]{2,1,0:T(2,128)(2,1)} %reshape.530), calls=%async_computation.1 | async-start | bytes 294912 | tf_op jit(solution)/shard_map/all_to_all | solution.py:125
  206.5 6.8 %multiply_convert_fusion.1 = (bf16[9,256,96]{1,2,0:T(8,128)(2,1)S(1)}, bf16[9,256,96]{1,2,0:T(8,128)(2,1)S(1)}) fusion(f32[96]{0:T(128)S(1)} %get-tuple-element.51, f32[9,256]{1,0:T(8,128)S(1)} %convert_add_fusion, f32[96]{0:T(128)S(1)} %sqrt.38, f32[96]{0:T(128)S(1)} %get-tuple-element.50), kind=kLoop, calls=%fused_computation.15 | loop fusion | flops 3760128 | bytes 895104 | tf_op jit(solution)/shard_map/convert.3
  213.4 0.2 convert_reduce_fusion
  213.6 14.5 %reshape.531 = bf16[24576,1,3]{2,1,0:T(2,128)(2,1)} reshape(bf16[16,2,2304]{2,1,0:T(2,128)(2,1)S(1)} %all-to-all-done.1) | data formatting | bytes 294912
  228.0 23.3 %copy.84 = bf16[3,1,24576]{2,0,1:T(4,128)(2,1)S(1)} copy(bf16[3,1,24576]{0,1,2:T(2,128)(2,1)} %bitcast.151) | data formatting | bytes 294912 | tf_op jit(solution)/shard_map/all_to_all | solution.py:125
  251.4 0.2 reshape.526
  251.6 0.6 fusion.5
  252.2 0.4 slice_bitcast_fusion.8
  252.7 0.5 pad_add_fusion
  253.2 0.1 reshape.523
  253.4 3.1 collective-permute-start.2
  256.6 2.2 collective-permute-start.3
  258.8 5.2 %collective-permute-done.3 = bf16[3,16,1024]{2,1,0:T(8,128)(2,1)S(1)} collective-permute-done((bf16[3,16,1024]{2,1,0:T(8,128)(2,1)S(1)}, bf16[3,16,1024]{2,1,0:T(8,128)(2,1)S(1)}, u32[]{:S(2)}, u32[]{:S(2)}) %collective-permute-start.3) | collective-permute-done | bytes 98336 | tf_op jit(solution)/shard_map/ppermute | solution.py:31
  264.1 0.5 fusion
  264.6 0.7 copy.93
  265.3 75.1 %all_to_all.23 = bf16[3,64,2048]{2,0,1:T(4,128)(2,1)S(1)} all-to-all(bf16[3,64,2048]{2,0,1:T(4,128)(2,1)S(1)} %copy.93), channel_id=1, replica_groups=mesh['space'=32,'tm'=16] {'space'}, dimensions={1} | all-to-all | bytes 1572864 | tf_op jit(solution)/shard_map/all_to_all | solution.py:150
  340.4 1.5 copy.94
  (24 shorter events, 0.5 us)
Async XLA Ops:
  0.0 9.9 %copy-start = (s32[16,2]{0,1:T(2,128)S(1)}, s32[16,2]{0,1:T(2,128)}, u32[]{:S(2)}) copy-start(s32[16,2]{0,1:T(2,128)} %param.10) | copy-start | bytes 388
  1.1 16.8 %collective-permute-start = (bf16[2,3,16,1024]{3,2,1,0:T(8,128)(2,1)S(1)}, bf16[2,3,16,1024]{3,2,1,0:T(8,128)(2,1)S(1)}, u32[]{:S(2)}, u32[]{:S(2)}) collective-permute-start(bf16[2,3,16,1024]{3,2,1,0:T(8,128)(2,1)S(1)} %get-tuple-element.42), channel_id=1, source_target_pairs={{0,1},{1,2},{2,3},{3,4},{4,5},{5,6},{6,7},{7,8},{8,9},{9,10},{10,1... | collective-permute-start | bytes 589832 | tf_op jit(solution)/shard_map/ppermute | solution.py:20
  3.9 14.1 %collective-permute-start.1 = (bf16[2,3,16,1024]{3,2,1,0:T(8,128)(2,1)S(1)}, bf16[2,3,16,1024]{3,2,1,0:T(8,128)(2,1)S(1)}, u32[]{:S(2)}, u32[]{:S(2)}) collective-permute-start(bf16[2,3,16,1024]{3,2,1,0:T(8,128)(2,1)S(1)} %get-tuple-element.43), channel_id=1, source_target_pairs={{1,0},{2,1},{3,2},{4,3},{5,4},{6,5},{7,6},{8,7},{9,8},{10,9},{11,1... | collective-permute-start | bytes 589832 | tf_op jit(solution)/shard_map/ppermute | solution.py:23
  22.6 12.3 %all-to-all-start = ((bf16[2,3,16,1536]{3,0,1,2:T(2,128)(2,1)}), bf16[2,3,16,1536]{3,0,1,2:T(2,128)(2,1)S(1)}, u32[]{:S(2)}, u32[]{:S(2)}) async-start(bf16[2,3,16,1536]{3,0,1,2:T(2,128)(2,1)} %copy.78), calls=%async_computation | async-start | bytes 589824 | tf_op jit(solution)/shard_map/all_to_all | solution.py:120
  191.1 22.3 %copy-start.1 = (s32[16,1]{0,1:T(1,128)S(1)}, s32[16,1]{0,1:T(1,128)}, u32[]{:S(2)}) copy-start(s32[16,1]{0,1:T(1,128)} %param.9) | copy-start | bytes 196
  201.1 12.5 %all-to-all-start.1 = ((bf16[16,2,2304]{2,1,0:T(2,128)(2,1)}), bf16[16,2,2304]{2,1,0:T(2,128)(2,1)S(1)}, u32[]{:S(2)}, u32[]{:S(2)}) async-start(bf16[16,2,2304]{2,1,0:T(2,128)(2,1)} %reshape.530), calls=%async_computation.1 | async-start | bytes 294912 | tf_op jit(solution)/shard_map/all_to_all | solution.py:125
  253.4 5.4 %collective-permute-start.2 = (bf16[3,16,1024]{2,1,0:T(8,128)(2,1)S(1)}, bf16[3,16,1024]{2,1,0:T(8,128)(2,1)S(1)}, u32[]{:S(2)}, u32[]{:S(2)}) collective-permute-start(bf16[3,16,1024]{2,1,0:T(8,128)(2,1)S(1)} %get-tuple-element.41), channel_id=1, source_target_pairs={{0,1},{1,2},{2,3},{3,4},{4,5},{5,6},{6,7},{7,8},{8,9},{9,10},{10,1... | collective-permute-start | bytes 294920 | tf_op jit(solution)/shard_map/ppermute | solution.py:31
  256.6 7.5 %collective-permute-start.3 = (bf16[3,16,1024]{2,1,0:T(8,128)(2,1)S(1)}, bf16[3,16,1024]{2,1,0:T(8,128)(2,1)S(1)}, u32[]{:S(2)}, u32[]{:S(2)}) collective-permute-start(bf16[3,16,1024]{2,1,0:T(8,128)(2,1)S(1)} %get-tuple-element.40), channel_id=1, source_target_pairs={{1,0},{2,1},{3,2},{4,3},{5,4},{6,5},{7,6},{8,7},{9,8},{10,9},{11,1... | collective-permute-start | bytes 294920 | tf_op jit(solution)/shard_map/ppermute | solution.py:31
where the time goes:
time: 343 us; the launch traced here: 342 us
  other arithmetic  157 us (46%)
  local copies, waits for them, and re-layouts  75.3 us (22%)
  blocking collectives  75.1 us (22%)
  starting transfers between devices  22.7 us (7%)
  waiting for transfers between devices  9.61 us (3%)
    unnamed x1, other arithmetic  135 us
    all_to_all x1, blocking collectives, on_device(): lax.all_to_all(outgoing, 'space', split_axis=1, concat_axis=1, tiled=True)  75.1 us
    unnamed x16, local copies, waits for them, and re-layouts  26 us
    all_to_all x1, local copies, waits for them, and re-layouts, on_device(): lax.all_to_all(adjoint_local, 'tm', split_axis=2, concat_axis=1, tiled=True)  23.3 us
    convert_element_type x2, local copies, waits for them, and re-layouts, misfit(): joined.reshape(joined.shape[:2] + (joined.shape[2] * joined.shape[3],))  19.7 us
    another operation x4, other arithmetic  13.9 us
  transfers between devices with their start and end apart: 6, of which 2 were waited for; matrix products, arithmetic and copies ran while one was open for 6% of the time, Pallas kernels for 0%

commit v1 on v0

--- a/solution.py
+++ b/solution.py
@@ -122,7 +122,19 @@
     frames_all = pieces.shape[3] // width
     local_coefs = pieces.astype(jnp.float32).reshape(2, items, rec_group, frames_all, width)
     adjoint_local = misfit(local_coefs, weight)
-    adjoint_back = lax.all_to_all(adjoint_local, "tm", split_axis=2, concat_axis=1, tiled=True)
+
+    def sector_choose(at_axis, pos_dim, obj):
+        return jnp.concatenate(
+            lax.all_to_all(
+                jnp.stack(jnp.split(obj, lax.axis_size("tm"), axis=at_axis), axis=0),
+                axis_name="tm",
+                concat_axis=0,
+                split_axis=0,
+            ),
+            axis=pos_dim,
+        )
+
+    adjoint_back = sector_choose(2, 1, adjoint_local)
     adjoint_frames = adjoint_back.reshape(comps, rec_dev, frames_dev, width)
     ext = synthesise(adjoint_frames, table, frames_dev)
     flat = ext.reshape(comps, rec_dev, (frames_dev + 2 * margin) * HOP)

time: 343 us -> 149 us (0.43)
  other arithmetic: 157 us -> 21.6 us
  local copies, waits for them, and re-layouts: 75.3 us -> 17.2 us
    unnamed x1 -> x0, other arithmetic: 135 us -> none
    all_to_all x1 -> x0, local copies, waits for them, and re-layouts: 23.3 us -> none  [on_device(): lax.all_to_all(adjoint_local, 'tm', split_axis=2, concat_axis=1, tiled=True)]
    convert_element_type x2 -> x1, local copies, waits for them, and re-layouts: 19.7 us -> 0.25 us  [misfit(): joined.reshape(joined.shape[:2] + (joined.shape[2] * joined.shape[3],))]
    unnamed x16 -> x28, local copies, waits for them, and re-layouts: 26 us -> 10.1 us
  transfers between devices with their start and end apart: 6 -> 6, of which waited for: 2 -> 2; matrix products, arithmetic and copies ran while one was open for 6% -> 13% of each run, Pallas kernels for 0% -> 0%
where the time goes in v1:
time: 149 us
  blocking collectives  75.1 us (50%)
  starting transfers between devices  22.8 us (15%)
  other arithmetic  21.6 us (14%)
  local copies, waits for them, and re-layouts  17.2 us (12%)
  waiting for transfers between devices  9.59 us (6%)
  matrix products  2.21 us (1%)
    all_to_all x1, blocking collectives, on_device(): lax.all_to_all(outgoing, 'space', split_axis=1, concat_axis=1, tiled=True)  75.1 us
    another operation x4, other arithmetic  13.9 us
    unnamed x28, local copies, waits for them, and re-layouts  10.1 us
    all_to_all x1, starting transfers between devices, on_device(): lax.all_to_all(packed, 'tm', split_axis=2, concat_axis=3, tiled=True)  6.74 us
    all_to_all x1, starting transfers between devices, sector_choose(): lax.all_to_all(jnp.stack(jnp.split(obj, lax.axis_size('tm'), axis=at_axis...  5.5 us
    ppermute x2, starting transfers between devices, shifted(): return lax.ppermute(block, axis, route)  5.28 us
    ppermute x2, waiting for transfers between devices, shifted(): return lax.ppermute(block, axis, route)  5.25 us
    all_to_all x1, waiting for transfers between devices, on_device(): lax.all_to_all(packed, 'tm', split_axis=2, concat_axis=3, tiled=True)  4.34 us
  transfers between devices with their start and end apart: 6, of which 2 were waited for; matrix products, arithmetic and copies ran while one was open for 13% of the time, Pallas kernels for 0%

profile of v1, /device:TPU:25, one launch (start us, length us, event | category | flops | bytes accessed | tf_op | source)
XLA Modules:
  0.0 149.0 jit_solution(8929880964629543283)
XLA Ops:
  0.0 1.1 fusion.24
  1.1 2.8 %collective-permute-start = (bf16[2,3,16,1024]{3,2,1,0:T(8,128)(2,1)S(1)}, bf16[2,3,16,1024]{3,2,1,0:T(8,128)(2,1)S(1)}, u32[]{:S(2)}, u32[]{:S(2)}) collective-permute-start(bf16[2,3,16,1024]{3,2,1,0:T(8,128)(2,1)S(1)} %get-tuple-element.42), channel_id=1, source_target_pairs={{0,1},{1,2},{2,3},{3,4},{4,5},{5,6},{6,7},{7,8},{8,9},{9,10},{10,1... | collective-permute-start | bytes 589832 | tf_op jit(solution)/shard_map/ppermute | solution.py:20
  3.9 2.5 %collective-permute-start.1 = (bf16[2,3,16,1024]{3,2,1,0:T(8,128)(2,1)S(1)}, bf16[2,3,16,1024]{3,2,1,0:T(8,128)(2,1)S(1)}, u32[]{:S(2)}, u32[]{:S(2)}) collective-permute-start(bf16[2,3,16,1024]{3,2,1,0:T(8,128)(2,1)S(1)} %get-tuple-element.43), channel_id=1, source_target_pairs={{1,0},{2,1},{3,2},{4,3},{5,4},{6,5},{7,6},{8,7},{9,8},{10,9},{11,1... | collective-permute-start | bytes 589832 | tf_op jit(solution)/shard_map/ppermute | solution.py:23
  6.4 3.4 %multiply_reduce_fusion = f32[96]{0:T(128)S(1)} fusion(f32[96]{0:T(128)S(1)} %get-tuple-element.50, f32[2304]{0:T(1024)S(1)} %convert_add_fusion.1), kind=kLoop, calls=%fused_computation.20 | loop fusion | flops 1990560 | bytes 9984 | tf_op jit(solution)/shard_map/reduce_sum | solution.py:43
  9.9 0.6 fusion.25
  10.5 6.6 %multiply_convert_fusion.3 = (bf16[2304,96]{0,1:T(8,128)(2,1)S(1)}, bf16[2304,96]{0,1:T(8,128)(2,1)S(1)}) fusion(f32[96]{0:T(128)S(1)} %get-tuple-element.51, f32[2304]{0:T(1024)S(1)} %convert_add_fusion.1, f32[96]{0:T(128)S(1)} %sqrt.38, f32[96]{0:T(128)S(1)} %get-tuple-element.50), kind=kLoop, calls=%fused_computation.19 | loop fusion | flops 3760128 | bytes 895104 | tf_op jit(solution)/shard_map/convert.7
  17.2 0.7 fusion.19
  17.9 1.1 pad_maximum_fusion
  20.1 1.1 convolution_convert_fusion.1
  21.2 0.3 reshape.517
  21.5 1.0 copy.91
  22.5 6.7 %all-to-all-start = ((bf16[2,3,16,1536]{3,0,1,2:T(2,128)(2,1)}), bf16[2,3,16,1536]{3,0,1,2:T(2,128)(2,1)S(1)}, u32[]{:S(2)}, u32[]{:S(2)}) async-start(bf16[2,3,16,1536]{3,0,1,2:T(2,128)(2,1)} %copy.91), calls=%async_computation | async-start | bytes 589824 | tf_op jit(solution)/shard_map/all_to_all | solution.py:120
  29.3 1.3 and_convert_fusion
  30.6 4.3 %all-to-all-done = bf16[2,3,16,1536]{3,0,1,2:T(2,128)(2,1)S(1)} async-done(((bf16[2,3,16,1536]{3,0,1,2:T(2,128)(2,1)}), bf16[2,3,16,1536]{3,0,1,2:T(2,128)(2,1)S(1)}, u32[]{:S(2)}, u32[]{:S(2)}) %all-to-all-start) | async-done | bytes 294944 | tf_op jit(solution)/shard_map/all_to_all | solution.py:120
  35.0 0.2 reshape.520
  35.3 0.2 fusion.22
  35.5 0.4 subtract_convert_fusion.1
  36.0 0.2 convert_element_type.135
  36.3 0.6 constant_dynamic-update-slice_fusion.15
  36.9 0.6 constant_dynamic-update-slice_fusion.14
  37.5 0.6 constant_dynamic-update-slice_fusion.13
  38.1 0.6 constant_dynamic-update-slice_fusion.12
  38.7 0.6 constant_dynamic-update-slice_fusion.11
  39.3 0.6 constant_dynamic-update-slice_fusion.10
  39.9 0.6 constant_dynamic-update-slice_fusion.9
  40.5 0.6 constant_dynamic-update-slice_fusion.8
  41.1 0.6 constant_dynamic-update-slice_fusion.7
  41.7 0.6 constant_dynamic-update-slice_fusion.6
  42.3 0.6 constant_dynamic-update-slice_fusion.5
  42.9 0.6 constant_dynamic-update-slice_fusion.4
  43.5 0.6 constant_dynamic-update-slice_fusion.3
  44.1 0.6 constant_dynamic-update-slice_fusion.2
  44.7 0.6 constant_dynamic-update-slice_fusion.1
  45.3 0.6 constant_dynamic-update-slice_fusion
  46.0 5.5 %all-to-all-start.1 = ((bf16[16,3,1,1536]{3,1,2,0:T(4,128)(2,1)}), bf16[16,3,1,1536]{3,1,2,0:T(4,128)(2,1)S(1)}, u32[]{:S(2)}, u32[]{:S(2)}) async-start(bf16[16,3,1,1536]{3,1,2,0:T(4,128)(2,1)} %constant_dynamic-update-slice_fusion), calls=%async_computation.1 | async-start | bytes 393216 | tf_op jit(solution)/shard_map/all_to_all | solution.py:128
  51.5 6.8 %multiply_convert_fusion.1 = (bf16[9,256,96]{1,2,0:T(8,128)(2,1)S(1)}, bf16[9,256,96]{1,2,0:T(8,128)(2,1)S(1)}) fusion(f32[96]{0:T(128)S(1)} %get-tuple-element.51, f32[9,256]{1,0:T(8,128)S(1)} %convert_add_fusion, f32[96]{0:T(128)S(1)} %sqrt.38, f32[96]{0:T(128)S(1)} %get-tuple-element.50), kind=kLoop, calls=%fused_computation.15 | loop fusion | flops 3760128 | bytes 895104 | tf_op jit(solution)/shard_map/convert.3
  58.3 0.2 convert_reduce_fusion
  58.5 0.2 reshape.522
  58.7 0.6 fusion.5
  59.3 0.4 slice_bitcast_fusion.8
  59.8 0.5 pad_add_fusion
  60.6 3.1 %collective-permute-start.2 = (bf16[3,16,1024]{2,1,0:T(8,128)(2,1)S(1)}, bf16[3,16,1024]{2,1,0:T(8,128)(2,1)S(1)}, u32[]{:S(2)}, u32[]{:S(2)}) collective-permute-start(bf16[3,16,1024]{2,1,0:T(8,128)(2,1)S(1)} %get-tuple-element.41), channel_id=1, source_target_pairs={{0,1},{1,2},{2,3},{3,4},{4,5},{5,6},{6,7},{7,8},{8,9},{9,10},{10,1... | collective-permute-start | bytes 294920 | tf_op jit(solution)/shard_map/ppermute | solution.py:31
  63.7 2.2 %collective-permute-start.3 = (bf16[3,16,1024]{2,1,0:T(8,128)(2,1)S(1)}, bf16[3,16,1024]{2,1,0:T(8,128)(2,1)S(1)}, u32[]{:S(2)}, u32[]{:S(2)}) collective-permute-start(bf16[3,16,1024]{2,1,0:T(8,128)(2,1)S(1)} %get-tuple-element.40), channel_id=1, source_target_pairs={{1,0},{2,1},{3,2},{4,3},{5,4},{6,5},{7,6},{8,7},{9,8},{10,9},{11,1... | collective-permute-start | bytes 294920 | tf_op jit(solution)/shard_map/ppermute | solution.py:31
  65.9 5.2 %collective-permute-done.3 = bf16[3,16,1024]{2,1,0:T(8,128)(2,1)S(1)} collective-permute-done((bf16[3,16,1024]{2,1,0:T(8,128)(2,1)S(1)}, bf16[3,16,1024]{2,1,0:T(8,128)(2,1)S(1)}, u32[]{:S(2)}, u32[]{:S(2)}) %collective-permute-start.3) | collective-permute-done | bytes 98336 | tf_op jit(solution)/shard_map/ppermute | solution.py:31
  71.2 0.5 fusion
  71.7 0.7 copy.105
  72.4 75.1 %all_to_all.19 = bf16[3,64,2048]{2,0,1:T(4,128)(2,1)S(1)} all-to-all(bf16[3,64,2048]{2,0,1:T(4,128)(2,1)S(1)} %copy.105), channel_id=1, replica_groups=mesh['space'=32,'tm'=16] {'space'}, dimensions={1} | all-to-all | bytes 1572864 | tf_op jit(solution)/shard_map/all_to_all | solution.py:162
  147.5 1.5 copy.106
  (35 shorter events, 1.8 us)
Async XLA Ops:
  0.0 9.9 %copy-start = (s32[16,2]{0,1:T(2,128)S(1)}, s32[16,2]{0,1:T(2,128)}, u32[]{:S(2)}) copy-start(s32[16,2]{0,1:T(2,128)} %param.10) | copy-start | bytes 388
  1.1 16.8 %collective-permute-start = (bf16[2,3,16,1024]{3,2,1,0:T(8,128)(2,1)S(1)}, bf16[2,3,16,1024]{3,2,1,0:T(8,128)(2,1)S(1)}, u32[]{:S(2)}, u32[]{:S(2)}) collective-permute-start(bf16[2,3,16,1024]{3,2,1,0:T(8,128)(2,1)S(1)} %get-tuple-element.42), channel_id=1, source_target_pairs={{0,1},{1,2},{2,3},{3,4},{4,5},{5,6},{6,7},{7,8},{8,9},{9,10},{10,1... | collective-permute-start | bytes 589832 | tf_op jit(solution)/shard_map/ppermute | solution.py:20
  3.9 14.0 %collective-permute-start.1 = (bf16[2,3,16,1024]{3,2,1,0:T(8,128)(2,1)S(1)}, bf16[2,3,16,1024]{3,2,1,0:T(8,128)(2,1)S(1)}, u32[]{:S(2)}, u32[]{:S(2)}) collective-permute-start(bf16[2,3,16,1024]{3,2,1,0:T(8,128)(2,1)S(1)} %get-tuple-element.43), channel_id=1, source_target_pairs={{1,0},{2,1},{3,2},{4,3},{5,4},{6,5},{7,6},{8,7},{9,8},{10,9},{11,1... | collective-permute-start | bytes 589832 | tf_op jit(solution)/shard_map/ppermute | solution.py:23
  22.5 35.7 %copy-start.1 = (s32[16,1]{0,1:T(1,128)S(1)}, s32[16,1]{0,1:T(1,128)}, u32[]{:S(2)}) copy-start(s32[16,1]{0,1:T(1,128)} %param.9) | copy-start | bytes 196
  22.5 12.4 %all-to-all-start = ((bf16[2,3,16,1536]{3,0,1,2:T(2,128)(2,1)}), bf16[2,3,16,1536]{3,0,1,2:T(2,128)(2,1)S(1)}, u32[]{:S(2)}, u32[]{:S(2)}) async-start(bf16[2,3,16,1536]{3,0,1,2:T(2,128)(2,1)} %copy.91), calls=%async_computation | async-start | bytes 589824 | tf_op jit(solution)/shard_map/all_to_all | solution.py:120
  46.0 12.5 %all-to-all-start.1 = ((bf16[16,3,1,1536]{3,1,2,0:T(4,128)(2,1)}), bf16[16,3,1,1536]{3,1,2,0:T(4,128)(2,1)S(1)}, u32[]{:S(2)}, u32[]{:S(2)}) async-start(bf16[16,3,1,1536]{3,1,2,0:T(4,128)(2,1)} %constant_dynamic-update-slice_fusion), calls=%async_computation.1 | async-start | bytes 393216 | tf_op jit(solution)/shard_map/all_to_all | solution.py:128
  60.6 5.4 %collective-permute-start.2 = (bf16[3,16,1024]{2,1,0:T(8,128)(2,1)S(1)}, bf16[3,16,1024]{2,1,0:T(8,128)(2,1)S(1)}, u32[]{:S(2)}, u32[]{:S(2)}) collective-permute-start(bf16[3,16,1024]{2,1,0:T(8,128)(2,1)S(1)} %get-tuple-element.41), channel_id=1, source_target_pairs={{0,1},{1,2},{2,3},{3,4},{4,5},{5,6},{6,7},{7,8},{8,9},{9,10},{10,1... | collective-permute-start | bytes 294920 | tf_op jit(solution)/shard_map/ppermute | solution.py:31
  63.7 7.5 %collective-permute-start.3 = (bf16[3,16,1024]{2,1,0:T(8,128)(2,1)S(1)}, bf16[3,16,1024]{2,1,0:T(8,128)(2,1)S(1)}, u32[]{:S(2)}, u32[]{:S(2)}) collective-permute-start(bf16[3,16,1024]{2,1,0:T(8,128)(2,1)S(1)} %get-tuple-element.40), channel_id=1, source_target_pairs={{1,0},{2,1},{3,2},{4,3},{5,4},{6,5},{7,6},{8,7},{9,8},{10,9},{11,1... | collective-permute-start | bytes 294920 | tf_op jit(solution)/shard_map/ppermute | solution.py:31
